TPU v7x, 128 devices: a whole 4x4x4 slice. The times are simulated.
128 devices in a mesh: row: 8 (over y, x_lo), col: 16 (over z, x_hi, core).
Axes of the slice: x: 4 (x_hi: 2, x_lo: 2; x = x_hi * 2 + x_lo), y: 4, z: 4, core: 2. Of those that a mesh axis runs over, the one named last changes fastest.
Arguments:
- blocks: bfloat16 [512, 32, 128, 128], P('row', 'col'), may hold values from -1.1953125 to 1.1953125
- columns: int32 [512, 32], replicated, may hold values from 0 to 31, as said below
Outputs:
- product: float32 [512, 32, 128, 128], P('row', 'col')
Inputs may be any that keep to these rules, and one draw needn't show every extreme that they name: `columns`: in every panel each block row and each block column holds exactly 2 nonzero blocks; the 2 column indices of one row within one panel are distinct.
All inputs are finite; a program needn't handle non-finite values.
Results may differ from a plain program's by a relative error of at most 0.0003.
Values may be sent and summed in bfloat16 or wider, within the bound.
A program may use at most 192 MiB of HBM per device.

v0:
```python
import jax
import jax.numpy as jnp
from jax import lax
from jax.sharding import PartitionSpec as P

STEPS = 3


def passed_along(block, axis, distance):
    devices = range(lax.axis_size(axis))
    route = [((i - distance) % len(devices), i) for i in devices]
    return lax.ppermute(block, axis, route)


def panel_product(left_blocks, left_cols, right_blocks, right_cols, target_cols):
    row_count = left_blocks.shape[0]
    slot_count = left_blocks.shape[1]
    block_size = left_blocks.shape[2]
    picked = jnp.take(right_blocks, left_cols, axis=0)
    picked_cols = jnp.take(right_cols, left_cols, axis=0)
    matches = picked_cols[:, None, :, :] == target_cols[:, :, None, None]
    products = jnp.einsum(
        "rfxy,rfgyz->rfgxz", left_blocks, picked, preferred_element_type=jnp.float32
    )
    placed = jnp.zeros((row_count, slot_count, block_size, block_size), jnp.float32)
    for first in range(slot_count):
        for second in range(slot_count):
            hit = matches[:, :, first, second][:, :, None, None]
            placed = placed + jnp.where(hit, products[:, first, second][:, None], 0.0)
    return placed


def skew_cols(panel_pair, amount):
    bit_count = (lax.axis_size("row") - 1).bit_length()
    for bit_index in range(bit_count):
        shifted = passed_along(panel_pair, "col", -(2 ** (bit_index + 1)))
        panel_pair = jnp.where(amount // 2**bit_index % 2 == 1, shifted, panel_pair)
    return panel_pair


def skew_rows(panel_pair, amount):
    bit_count = (lax.axis_size("row") - 1).bit_length()
    for bit_index in range(bit_count):
        shifted = passed_along(panel_pair, "row", -(2**bit_index))
        panel_pair = jnp.where(amount // 2**bit_index % 2 == 1, shifted, panel_pair)
    return panel_pair


def slide_rows(panel_pair):
    leading = passed_along(panel_pair[0], "row", -1)
    return jnp.stack([panel_pair[1], leading])


def shards(blocks, columns):
    panel_rows = blocks.shape[0] // 2
    slot_count = blocks.shape[1]
    block_size = blocks.shape[2]
    panel_count = lax.axis_size("col")
    row_index = lax.axis_index("row")
    col_index = lax.axis_index("col")
    own_panels = blocks.reshape(2, panel_rows, slot_count, block_size, block_size)
    pattern = columns.reshape(panel_count, panel_rows, panel_count, slot_count)
    left_list = []
    right_list = []
    odd_panel = passed_along(own_panels[1], "col", -1)
    left_pair = skew_cols(jnp.stack([own_panels[0], odd_panel]), row_index)
    left_list.append(left_pair)
    slid_pair = slide_rows(own_panels)
    right_pair = skew_rows(jnp.where(col_index % 2 == 1, slid_pair, own_panels), col_index // 2)
    right_list.append(right_pair)
    for step_index in range(1, STEPS):
        left_pair = passed_along(left_pair, "col", -1)
        right_pair = slide_rows(right_pair)
        left_list.append(left_pair)
        right_list.append(right_pair)
    totals = []
    for member in range(2):
        panel_row = 2 * row_index + member
        target = pattern[panel_row, :, col_index]
        running = jnp.zeros((panel_rows, slot_count, block_size, block_size), jnp.float32)
        for step_index in range(STEPS):
            inner_panel = (panel_row + col_index + step_index) % panel_count
            running = running + panel_product(
                left_list[step_index][member],
                pattern[panel_row, :, inner_panel],
                right_list[step_index][member],
                pattern[inner_panel, :, col_index],
                target,
            )
        totals.append(running)
    return jnp.stack(totals).reshape(2 * panel_rows, slot_count, block_size, block_size)


def solution(mesh):
    in_specs = (P("row", "col", None, None), P())
    out_specs = P("row", "col", None, None)
    return jax.shard_map(shards, mesh=mesh, in_specs=in_specs, out_specs=out_specs, check_vma=False)
```

profile of v0, /device:TPU:1, one launch (start us, length us, event | category | flops | bytes accessed | tf_op | source)
XLA Modules:
  0.0 688.8 jit_solution(5709511416588726373)
XLA Ops:
  0.0 6.9 %slice_bitcast_fusion.62 = (bf16[1,32,2,128,128]{4,3,2,1,0:T(8,128)(2,1)S(1)}, bf16[1,32,2,128,128]{4,3,2,1,0:T(8,128)(2,1)}, bf16[32,2,128,128]{3,2,1,0:T(8,128)(2,1)S(1)}, bf16[32,2,128,128]{3,2,1,0:T(8,128)(2,1)}) fusion(bf16[64,2,128,128]{3,2,1,0:T(8,128)(2,1)} %param.6), kind=kLoop, calls=%fused_computation.159 | loop fusion | bytes 12582912 | tf_op jit(solution)/shard_map/slice | solution.py:50
  8.3 26.4 %collective-permute-done.4 = bf16[32,2,128,128]{3,2,1,0:T(8,128)(2,1)S(1)} collective-permute-done((bf16[32,2,128,128]{3,2,1,0:T(8,128)(2,1)S(1)}, bf16[32,2,128,128]{3,2,1,0:T(8,128)(2,1)S(1)}, u32[]{:S(2)}, u32[]{:S(2)}) %collective-permute-start.4) | collective-permute-done | bytes 2097184 | tf_op jit(solution)/shard_map/ppermute | solution.py:12
  37.4 8.3 %collective-permute-start.5 = (bf16[2,32,2,128,128]{4,3,2,1,0:T(8,128)(2,1)}, bf16[2,32,2,128,128]{4,3,2,1,0:T(8,128)(2,1)}, u32[]{:S(2)}, u32[]{:S(2)}) collective-permute-start(bf16[2,32,2,128,128]{4,3,2,1,0:T(8,128)(2,1)} %pad_maximum_fusion.1), channel_id=1, source_target_pairs={{2,0},{3,1},{4,2},{5,3},{6,4},{7,5},{8,6},{9,7},{10,8},{11,9},{12,... | collective-permute-start | bytes 12582920 | tf_op jit(solution)/shard_map/ppermute | solution.py:12
  48.5 130.1 %collective-permute-done = bf16[32,2,128,128]{3,2,1,0:T(8,128)(2,1)} collective-permute-done((bf16[32,2,128,128]{3,2,1,0:T(8,128)(2,1)}, bf16[32,2,128,128]{3,2,1,0:T(8,128)(2,1)}, u32[]{:S(2)}, u32[]{:S(2)}) %collective-permute-start) | collective-permute-done | bytes 2097184 | tf_op jit(solution)/shard_map/ppermute | solution.py:12
  178.5 3.8 maximum_select_fusion
  184.8 3.4 broadcast_select_fusion
  188.4 85.6 %collective-permute-done.1 = bf16[2,32,2,128,128]{4,3,2,1,0:T(8,128)(2,1)} collective-permute-done((bf16[2,32,2,128,128]{4,3,2,1,0:T(8,128)(2,1)}, bf16[2,32,2,128,128]{4,3,2,1,0:T(8,128)(2,1)}, u32[]{:S(2)}, u32[]{:S(2)}) %collective-permute-start.1) | collective-permute-done | bytes 4194336 | tf_op jit(solution)/shard_map/ppermute | solution.py:12
  274.0 3.8 broadcast_select_fusion.3
  280.6 3.5 broadcast_select_fusion.1
  289.3 81.3 %collective-permute-done.2 = bf16[2,32,2,128,128]{4,3,2,1,0:T(8,128)(2,1)} collective-permute-done((bf16[2,32,2,128,128]{4,3,2,1,0:T(8,128)(2,1)}, bf16[2,32,2,128,128]{4,3,2,1,0:T(8,128)(2,1)}, u32[]{:S(2)}, u32[]{:S(2)}) %collective-permute-start.2) | collective-permute-done | bytes 4194336 | tf_op jit(solution)/shard_map/ppermute | solution.py:12
  370.6 4.6 broadcast_select_fusion.4
  377.8 4.6 broadcast_select_fusion.2
  390.5 77.6 %collective-permute-done.3 = bf16[2,32,2,128,128]{4,3,2,1,0:T(8,128)(2,1)} collective-permute-done((bf16[2,32,2,128,128]{4,3,2,1,0:T(8,128)(2,1)}, bf16[2,32,2,128,128]{4,3,2,1,0:T(8,128)(2,1)}, u32[]{:S(2)}, u32[]{:S(2)}) %collective-permute-start.3) | collective-permute-done | bytes 4194336 | tf_op jit(solution)/shard_map/ppermute | solution.py:12
  472.5 16.6 %collective-permute-start.9 = (bf16[32,2,128,128]{3,2,1,0:T(8,128)(2,1)}, bf16[32,2,128,128]{3,2,1,0:T(8,128)(2,1)}, u32[]{:S(2)}, u32[]{:S(2)}) collective-permute-start(bf16[32,2,128,128]{3,2,1,0:T(8,128)(2,1)} %get-tuple-element.31), channel_id=1, source_target_pairs={{16,0},{32,16},{48,32},{64,48},{80,64},{96,80},{112,96},{0,112},{1... | collective-permute-start | bytes 6291464 | tf_op jit(solution)/shard_map/ppermute | solution.py:12
  489.2 4.7 gather_fusion.1
  493.9 3.0 gather_fusion.3
  496.9 3.1 gather_fusion.7
  500.0 6.5 copy.142
  506.5 6.5 copy.124
  515.1 4.2 fusion.18
  519.2 3.4 slice_bitcast_fusion.34
  525.5 3.0 copy.127
  534.3 6.5 copy.179
  540.8 4.2 fusion.27
  545.0 3.5 slice_bitcast_fusion.15
  548.5 2.9 copy.180
  557.2 2.9 copy.186
  560.1 4.7 gather_fusion.5
  564.8 6.5 copy.160
  571.3 4.7 gather_fusion.9
  576.0 6.4 copy.197
  582.4 4.7 gather_fusion.11
  587.1 6.4 copy.215
  593.5 4.2 fusion.21
  597.7 2.9 slice_bitcast_fusion.27
  600.6 2.9 copy.143
  603.6 2.9 copy.145
  606.5 2.9 copy.147
  611.3 4.2 fusion.30
  618.4 3.0 copy.198
  624.2 2.9 copy.202
  629.0 4.2 fusion.24
  646.6 4.2 fusion.33
  653.6 2.9 copy.216
  658.4 3.1 copy.220
  664.4 12.9 %add_add_fusion.1 = f32[1,32,2,128,128]{4,3,2,1,0:T(8,128)S(1)} fusion(f32[32,128,128]{2,1,0:T(8,128)} %copy.167, f32[32,128,128]{2,1,0:T(8,128)} %copy.165, f32[32,128,128]{2,1,0:T(8,128)} %copy.163, f32[32,128,128]{2,1,0:T(8,128)} %copy.161, f32[32,128,128]{2,1,0:T(8,128)} %copy.149, f32[32,128,128]{2,1,0:T(8,128)} %copy.147, f32[32,128,128]{2,1,0:T(8,128)} %copy.145, ...), kind=kLoop, calls=%fused_computation.28 | loop fusion | flops 24117248 | bytes 29360896 | tf_op jit(solution)/shard_map/add | solution.py:83
  679.5 4.9 add_add_fusion
  684.4 4.0 pad_maximum_fusion
  (163 shorter events, 81.5 us)
Async XLA Ops:
  6.9 27.9 %collective-permute-start.4 = (bf16[32,2,128,128]{3,2,1,0:T(8,128)(2,1)S(1)}, bf16[32,2,128,128]{3,2,1,0:T(8,128)(2,1)S(1)}, u32[]{:S(2)}, u32[]{:S(2)}) collective-permute-start(bf16[32,2,128,128]{3,2,1,0:T(8,128)(2,1)S(1)} %get-tuple-element.35), channel_id=1, source_target_pairs={{1,0},{2,1},{3,2},{4,3},{5,4},{6,5},{7,6},{8,7},{9,8},{10,9},{11,1... | collective-permute-start | bytes 6291464 | tf_op jit(solution)/shard_map/ppermute | solution.py:12
  34.8 2.7 copy-start
  37.4 147.4 %collective-permute-start.5 = (bf16[2,32,2,128,128]{4,3,2,1,0:T(8,128)(2,1)}, bf16[2,32,2,128,128]{4,3,2,1,0:T(8,128)(2,1)}, u32[]{:S(2)}, u32[]{:S(2)}) collective-permute-start(bf16[2,32,2,128,128]{4,3,2,1,0:T(8,128)(2,1)} %pad_maximum_fusion.1), channel_id=1, source_target_pairs={{2,0},{3,1},{4,2},{5,3},{6,4},{7,5},{8,6},{9,7},{10,8},{11,9},{12,... | collective-permute-start | bytes 12582920 | tf_op jit(solution)/shard_map/ppermute | solution.py:12
  45.7 132.9 %collective-permute-start = (bf16[32,2,128,128]{3,2,1,0:T(8,128)(2,1)}, bf16[32,2,128,128]{3,2,1,0:T(8,128)(2,1)}, u32[]{:S(2)}, u32[]{:S(2)}) collective-permute-start(bf16[32,2,128,128]{3,2,1,0:T(8,128)(2,1)} %get-tuple-element.36), channel_id=1, source_target_pairs={{16,0},{32,16},{48,32},{64,48},{80,64},{96,80},{112,96},{0,112},{1... | collective-permute-start | bytes 6291464 | tf_op jit(solution)/shard_map/ppermute | solution.py:12
  182.4 91.6 %collective-permute-start.1 = (bf16[2,32,2,128,128]{4,3,2,1,0:T(8,128)(2,1)}, bf16[2,32,2,128,128]{4,3,2,1,0:T(8,128)(2,1)}, u32[]{:S(2)}, u32[]{:S(2)}) collective-permute-start(bf16[2,32,2,128,128]{4,3,2,1,0:T(8,128)(2,1)} %maximum_select_fusion), channel_id=1, source_target_pairs={{16,0},{32,16},{48,32},{64,48},{80,64},{96,80},{112,96},{0,112},{1... | collective-permute-start | bytes 12582920 | tf_op jit(solution)/shard_map/ppermute | solution.py:12
  188.2 92.3 %collective-permute-start.6 = (bf16[2,32,2,128,128]{4,3,2,1,0:T(8,128)(2,1)}, bf16[2,32,2,128,128]{4,3,2,1,0:T(8,128)(2,1)}, u32[]{:S(2)}, u32[]{:S(2)}) collective-permute-start(bf16[2,32,2,128,128]{4,3,2,1,0:T(8,128)(2,1)} %broadcast_select_fusion), channel_id=1, source_target_pairs={{4,0},{5,1},{6,2},{7,3},{8,4},{9,5},{10,6},{11,7},{12,8},{13,9},{1... | collective-permute-start | bytes 12582920 | tf_op jit(solution)/shard_map/ppermute | solution.py:12
  277.8 92.8 %collective-permute-start.2 = (bf16[2,32,2,128,128]{4,3,2,1,0:T(8,128)(2,1)}, bf16[2,32,2,128,128]{4,3,2,1,0:T(8,128)(2,1)}, u32[]{:S(2)}, u32[]{:S(2)}) collective-permute-start(bf16[2,32,2,128,128]{4,3,2,1,0:T(8,128)(2,1)} %broadcast_select_fusion.3), channel_id=1, source_target_pairs={{32,0},{48,16},{64,32},{80,48},{96,64},{112,80},{0,96},{16,112},{3... | collective-permute-start | bytes 12582920 | tf_op jit(solution)/shard_map/ppermute | solution.py:12
  280.6 4.4 copy-start.14
  284.0 93.7 %collective-permute-start.7 = (bf16[2,32,2,128,128]{4,3,2,1,0:T(8,128)(2,1)}, bf16[2,32,2,128,128]{4,3,2,1,0:T(8,128)(2,1)}, u32[]{:S(2)}, u32[]{:S(2)}) collective-permute-start(bf16[2,32,2,128,128]{4,3,2,1,0:T(8,128)(2,1)} %broadcast_select_fusion.1), channel_id=1, source_target_pairs={{8,0},{9,1},{10,2},{11,3},{12,4},{13,5},{14,6},{15,7},{0,8},{1,9},... | collective-permute-start | bytes 12582920 | tf_op jit(solution)/shard_map/ppermute | solution.py:12
  375.3 92.8 %collective-permute-start.3 = (bf16[2,32,2,128,128]{4,3,2,1,0:T(8,128)(2,1)}, bf16[2,32,2,128,128]{4,3,2,1,0:T(8,128)(2,1)}, u32[]{:S(2)}, u32[]{:S(2)}) collective-permute-start(bf16[2,32,2,128,128]{4,3,2,1,0:T(8,128)(2,1)} %broadcast_select_fusion.4), channel_id=1, source_target_pairs={{64,0},{80,16},{96,32},{112,48},{0,64},{16,80},{32,96},{48,112},{6... | collective-permute-start | bytes 12582920 | tf_op jit(solution)/shard_map/ppermute | solution.py:12
  382.3 130.6 %collective-permute-start.8 = (bf16[2,32,2,128,128]{4,3,2,1,0:T(8,128)(2,1)}, bf16[2,32,2,128,128]{4,3,2,1,0:T(8,128)(2,1)}, u32[]{:S(2)}, u32[]{:S(2)}) collective-permute-start(bf16[2,32,2,128,128]{4,3,2,1,0:T(8,128)(2,1)} %broadcast_select_fusion.2), channel_id=1, source_target_pairs={{1,0},{2,1},{3,2},{4,3},{5,4},{6,5},{7,6},{8,7},{9,8},{10,9},{11,1... | collective-permute-start | bytes 12582920 | tf_op jit(solution)/shard_map/ppermute | solution.py:12
  472.5 87.6 %collective-permute-start.9 = (bf16[32,2,128,128]{3,2,1,0:T(8,128)(2,1)}, bf16[32,2,128,128]{3,2,1,0:T(8,128)(2,1)}, u32[]{:S(2)}, u32[]{:S(2)}) collective-permute-start(bf16[32,2,128,128]{3,2,1,0:T(8,128)(2,1)} %get-tuple-element.31), channel_id=1, source_target_pairs={{16,0},{32,16},{48,32},{64,48},{80,64},{96,80},{112,96},{0,112},{1... | collective-permute-start | bytes 6291464 | tf_op jit(solution)/shard_map/ppermute | solution.py:12
  500.0 82.4 %collective-permute-start.11 = (bf16[32,2,128,128]{3,2,1,0:T(8,128)(2,1)S(1)}, bf16[32,2,128,128]{3,2,1,0:T(8,128)(2,1)}, u32[]{:S(2)}, u32[]{:S(2)}) collective-permute-start(bf16[32,2,128,128]{3,2,1,0:T(8,128)(2,1)S(1)} %get-tuple-element.32), channel_id=1, source_target_pairs={{16,0},{32,16},{48,32},{64,48},{80,64},{96,80},{112,96},{0,112},{1... | collective-permute-start | bytes 6291464 | tf_op jit(solution)/shard_map/ppermute | solution.py:12
  513.0 116.1 %collective-permute-start.10 = (bf16[2,32,2,128,128]{4,3,2,1,0:T(8,128)(2,1)}, bf16[2,32,2,128,128]{4,3,2,1,0:T(8,128)(2,1)}, u32[]{:S(2)}, u32[]{:S(2)}) collective-permute-start(bf16[2,32,2,128,128]{4,3,2,1,0:T(8,128)(2,1)} %collective-permute-done.8), channel_id=1, source_target_pairs={{1,0},{2,1},{3,2},{4,3},{5,4},{6,5},{7,6},{8,7},{9,8},{10,9},{11,1... | collective-permute-start | bytes 12582920 | tf_op jit(solution)/shard_map/ppermute | solution.py:12
  658.4 5.9 copy-start.4
  664.3 13.0 %copy-start.1 = (f32[32,128,128]{2,1,0:T(8,128)S(1)}, f32[32,128,128]{2,1,0:T(8,128)}, u32[]{:S(2)}) copy-start(f32[32,128,128]{2,1,0:T(8,128)} %copy.180) | copy-start | bytes 6291460
  664.3 13.0 %copy-start.2 = (f32[32,128,128]{2,1,0:T(8,128)S(1)}, f32[32,128,128]{2,1,0:T(8,128)}, u32[]{:S(2)}) copy-start(f32[32,128,128]{2,1,0:T(8,128)} %copy.182) | copy-start | bytes 6291460
  664.3 13.0 %copy-start.3 = (f32[32,128,128]{2,1,0:T(8,128)S(1)}, f32[32,128,128]{2,1,0:T(8,128)}, u32[]{:S(2)}) copy-start(f32[32,128,128]{2,1,0:T(8,128)} %copy.184) | copy-start | bytes 6291460
  664.3 13.0 %copy-start.5 = (f32[32,128,128]{2,1,0:T(8,128)S(1)}, f32[32,128,128]{2,1,0:T(8,128)}, u32[]{:S(2)}) copy-start(f32[32,128,128]{2,1,0:T(8,128)} %copy.186) | copy-start | bytes 6291460
  664.3 13.0 %copy-start.6 = (f32[32,128,128]{2,1,0:T(8,128)S(1)}, f32[32,128,128]{2,1,0:T(8,128)}, u32[]{:S(2)}) copy-start(f32[32,128,128]{2,1,0:T(8,128)} %copy.198) | copy-start | bytes 6291460
  664.4 13.0 %copy-start.7 = (f32[32,128,128]{2,1,0:T(8,128)S(1)}, f32[32,128,128]{2,1,0:T(8,128)}, u32[]{:S(2)}) copy-start(f32[32,128,128]{2,1,0:T(8,128)} %copy.200) | copy-start | bytes 6291460
  664.4 13.0 %copy-start.8 = (f32[32,128,128]{2,1,0:T(8,128)S(1)}, f32[32,128,128]{2,1,0:T(8,128)}, u32[]{:S(2)}) copy-start(f32[32,128,128]{2,1,0:T(8,128)} %copy.202) | copy-start | bytes 6291460
  664.4 13.0 %copy-start.9 = (f32[32,128,128]{2,1,0:T(8,128)S(1)}, f32[32,128,128]{2,1,0:T(8,128)}, u32[]{:S(2)}) copy-start(f32[32,128,128]{2,1,0:T(8,128)} %copy.204) | copy-start | bytes 6291460
  664.4 13.3 %copy-start.10 = (f32[32,128,128]{2,1,0:T(8,128)S(1)}, f32[32,128,128]{2,1,0:T(8,128)}, u32[]{:S(2)}) copy-start(f32[32,128,128]{2,1,0:T(8,128)} %copy.216) | copy-start | bytes 6291460
  664.4 13.9 %copy-start.11 = (f32[32,128,128]{2,1,0:T(8,128)S(1)}, f32[32,128,128]{2,1,0:T(8,128)}, u32[]{:S(2)}) copy-start(f32[32,128,128]{2,1,0:T(8,128)} %copy.218) | copy-start | bytes 6291460
  664.4 14.5 %copy-start.12 = (f32[32,128,128]{2,1,0:T(8,128)S(1)}, f32[32,128,128]{2,1,0:T(8,128)}, u32[]{:S(2)}) copy-start(f32[32,128,128]{2,1,0:T(8,128)} %copy.220) | copy-start | bytes 6291460
  664.4 15.0 %copy-start.13 = (f32[32,128,128]{2,1,0:T(8,128)S(1)}, f32[32,128,128]{2,1,0:T(8,128)}, u32[]{:S(2)}) copy-start(f32[32,128,128]{2,1,0:T(8,128)} %copy.222) | copy-start | bytes 6291460
where the time goes:
time: 698 us; the launch traced here: 689 us
  waiting for transfers between devices  401 us (57%)
  local copies, waits for them, and re-layouts  170 us (24%)
  other arithmetic  50.9 us (7%)
  starting transfers between devices  41 us (6%)
  matrix products  25 us (4%)
    ppermute x12, waiting for transfers between devices, passed_along(): return lax.ppermute(block, axis, route)  401 us
    broadcast_in_dim x60, local copies, waits for them, and re-layouts, panel_product(): placed = placed + jnp.where(hit, products[:, first, second][:, None], 0.0)  86.8 us
    gather x12, local copies, waits for them, and re-layouts, panel_product(): picked = jnp.take(right_blocks, left_cols, axis=0)  63.7 us
    ppermute x12, starting transfers between devices, passed_along(): return lax.ppermute(block, axis, route)  41 us
    dot_general x6, matrix products, panel_product(): jnp.einsum('rfxy,rfgyz->rfgxz', left_blocks, picked, preferred_element_ty...  25 us
    add x2, other arithmetic, shards(): running + panel_product(left_list[step_index][member], pattern[panel_row,...  17.8 us
  transfers between devices with their start and end apart: 12, of which 5 were waited for; matrix products, arithmetic and copies ran while one was open for 26% of the time, Pallas kernels for 0%

commit v1 on v0

v1 whole, which is shorter than its diff:
```python
import jax
import jax.numpy as jnp
from jax import lax
from jax.experimental import pallas as pl
from jax.experimental.pallas import tpu as pltpu
from jax.sharding import PartitionSpec as P

STEPS = 3
PB = 32
BS = 128
MESH = pl.DeviceIdType.MESH


def kernel(rows_n, cols_n, pattern, own, out, left, right0, right1, right2, right3, total, left_recv, right_recv, send_sem, out_sem):
    rights = (right0, right1, right2, right3)
    r = lax.axis_index("row")
    c = lax.axis_index("col")
    chips = cols_n // 2
    m = c // 2
    core = c % 2

    barrier = pltpu.get_barrier_semaphore()
    for step in range(1, cols_n):
        pl.semaphore_signal(barrier, inc=1, device_id=(r, (c + step) % cols_n), device_id_type=MESH)
    for step in range(1, rows_n):
        pl.semaphore_signal(barrier, inc=1, device_id=((r + step) % rows_n, c), device_id_type=MESH)
    pl.semaphore_wait(barrier, cols_n + rows_n - 2)

    def panel(member):
        return own.at[pl.ds(pl.multiple_of(member * PB, PB), PB)]

    def remote(source, target, arrived, index, device):
        return pltpu.make_async_remote_copy(
            src_ref=source, dst_ref=target, send_sem=send_sem.at[index], recv_sem=arrived,
            device_id=device, device_id_type=MESH,
        )

    sends = []

    def send(source, target, arrived, index, device):
        here = jnp.logical_and(device[0] == r, device[1] == c)

        @pl.when(here)
        def _():
            pltpu.make_async_copy(source, target, arrived).start()

        @pl.when(jnp.logical_not(here))
        def _():
            remote(source, target, arrived, index, device).start()

        sends.append((source, target, arrived, index, device, here))

    def chip_col(shift, which):
        return ((m - shift + 2 * chips) % chips) * 2 + which

    late = 1 - core
    first_slot = jnp.where(core == 0, 5, 3)
    plan = (
        (1, r + 2 * late, 1 - core, first_slot),
        (0, r, core, 0),
        (1, r + 1, core, 4),
        (0, r + 1, core, 2),
    )
    for index, (member, shift, which, slot) in enumerate(plan):
        send(panel(member), left.at[slot], left_recv.at[slot], index, (r, chip_col(shift, which)))
    for j in range(4):
        member = (c + j) % 2
        dest = ((2 * r + member - c - j + 4 * rows_n) // 2) % rows_n
        send(panel(member), rights[j], right_recv.at[j], 4 + j, (dest, c))

    def wait(target, arrived):
        pltpu.make_async_copy(target, target, arrived).wait()

    other = (r, c + 1 - 2 * core)
    outer = jnp.where(core == 0, 2, 0)
    relays = []
    for index, (source, target) in enumerate(((outer, 1), (4, 3 + 2 * core))):
        wait(left.at[source], left_recv.at[source])
        copy = remote(left.at[source], left.at[target], left_recv.at[target], 8 + index, other)
        copy.start()
        relays.append(copy)
    for slot in (2 - outer, 1, 3, 5):
        wait(left.at[slot], left_recv.at[slot])
    for j in range(4):
        wait(rights[j], right_recv.at[j])

    for member in range(2):
        panel_row = 2 * r + member

        def row(a, carry, member=member, panel_row=panel_row):
            line = panel_row * PB + a
            goals = [pattern[line, 2 * c + e] for e in range(2)]
            acc = jnp.zeros((BS, 2 * BS), jnp.float32)
            for step in range(STEPS):
                inner = (panel_row + c + step) % cols_n
                block = right_rows = rights[member + step]
                slot = member * STEPS + step
                lhs = jnp.concatenate([left[slot, a, 0], left[slot, a, 1]], axis=1)
                parts = []
                for f in range(2):
                    pick = pattern[line, 2 * inner + f]
                    held = [pattern[inner * PB + pick, 2 * c + g] for g in range(2)]
                    blocks = [block[pick, g] for g in range(2)]
                    zero = jnp.zeros_like(blocks[0])
                    parts.append(jnp.concatenate(
                        [jnp.where(held[0] == goals[e], blocks[0], jnp.where(held[1] == goals[e], blocks[1], zero)) for e in range(2)],
                        axis=1))
                acc = acc + jnp.dot(lhs, jnp.concatenate(parts, axis=0), preferred_element_type=jnp.float32)
            total[member * PB + a, 0] = acc[:, :BS]
            total[member * PB + a, 1] = acc[:, BS:]
            return carry

        lax.fori_loop(0, PB, row, 0)
        half = pl.ds(member * PB, PB)
        pltpu.make_async_copy(total.at[half], out.at[half], out_sem.at[member]).start()

    for source, target, arrived, index, device, here in sends:
        @pl.when(jnp.logical_not(here))
        def _(args=(source, target, arrived, index, device)):
            remote(*args).wait_send()
    for copy in relays:
        copy.wait_send()
    for member in range(2):
        half = pl.ds(member * PB, PB)
        pltpu.make_async_copy(total.at[half], out.at[half], out_sem.at[member]).wait()


def solution(mesh):
    rows_n, cols_n = mesh.shape["row"], mesh.shape["col"]

    def shards(blocks, columns):
        panel = pltpu.VMEM((PB, 2, BS, BS), jnp.bfloat16)

        def body(*refs):
            kernel(rows_n, cols_n, *refs)

        return pl.pallas_call(
            body,
            out_shape=jax.ShapeDtypeStruct(blocks.shape, jnp.float32),
            in_specs=[pl.BlockSpec(memory_space=pltpu.SMEM), pl.BlockSpec(memory_space=pl.ANY)],
            out_specs=pl.BlockSpec(memory_space=pl.ANY),
            scratch_shapes=[
                pltpu.VMEM((6, PB, 2, BS, BS), jnp.bfloat16),
                panel, panel, panel, panel,
                pltpu.VMEM((2 * PB, 2, BS, BS), jnp.float32),
                pltpu.SemaphoreType.DMA((6,)),
                pltpu.SemaphoreType.DMA((4,)),
                pltpu.SemaphoreType.DMA((10,)),
                pltpu.SemaphoreType.DMA((2,)),
            ],
            compiler_params=pltpu.CompilerParams(
                collective_id=0, has_side_effects=True, vmem_limit_bytes=56 * 2**20
            ),
        )(columns, blocks)

    return jax.shard_map(
        shards, mesh=mesh, in_specs=(P("row", "col", None, None), P()),
        out_specs=P("row", "col", None, None), check_vma=False,
    )
```

time: 698 us -> 229 us (0.33)
  the two profiles are of different devices: /device:TPU:1 before, /device:TPU:16 now
where the time goes in v1:
time: 229 us; the launch traced here: 228 us
  Pallas kernels  219 us (96%)
  local copies, waits for them, and re-layouts  9.56 us (4%)
    pallas_call x1, Pallas kernels, shards(): pl.pallas_call(body, out_shape=jax.ShapeDtypeStruct(blocks.shape, jnp.flo...  219 us
    unnamed x2, local copies, waits for them, and re-layouts  9.56 us

profile of v1, /device:TPU:16, one launch (start us, length us, event | category | flops | bytes accessed | tf_op | source)
XLA Modules:
  0.0 228.5 jit_solution(2758144103750888941)
XLA Ops:
  0.0 1.7 copy.3.refs_0_
  1.7 218.9 %shard_map.28 = f32[64,2,128,128]{3,2,1,0:T(8,128)} custom-call(s32[512,32]{1,0:T(8,128)} %copy.3.refs_0_, bf16[64,2,128,128]{3,2,1,0:T(8,128)(2,1)} %refs_1_.1), custom_call_target="tpu_custom_call" | custom-call | tf_op jit(solution)/shard_map/pallas_call | solution.py:137
  220.6 7.9 %copy.5 = f32[64,2,128,128]{3,2,1,0:T(8,128)} copy(f32[64,2,128,128]{3,2,1,0:T(8,128)} %shard_map.28) | data formatting | bytes 16777216

commit v2 on v1

v2 whole, which is shorter than its diff:
```python
import jax
import jax.numpy as jnp
from jax import lax
from jax.experimental import pallas as pl
from jax.experimental.pallas import tpu as pltpu
from jax.sharding import PartitionSpec as P

STEPS = 3
PB = 32
BS = 128
CHUNKS = 8
CR = PB // CHUNKS
MESH = pl.DeviceIdType.MESH

CHAIN_LEFT = ((2952, 152), (400, 9824))
CHAIN_RIGHT = ((356, 2184), (2208, 8800))


def bit(masks, parity, member, position, core):
    mask = jnp.where(parity == 0, masks[0][member], masks[1][member])
    return jnp.bitwise_and(jnp.right_shift(mask, position * 2 + core), 1) == 1


def near_far(start):
    return start + start % 2, start + 1 - start % 2


class Way:
    def __init__(self, r, m, core, member, rows_n, chips):
        start = r + (1 - core) if member == 1 else r
        self.left = []
        for shift in near_far(start):
            rel = 2 * (shift - r) + core
            which = core if member == 0 else rel // 3
            self.left.append((shift, (r, ((m - shift + 2 * chips) % chips) * 2 + which), 3 * member + rel - member - which))
        start = m + core if member == 0 else m
        self.right = []
        for shift in near_far(start):
            self.right.append((shift, ((r - shift + 2 * rows_n) % rows_n, 2 * m + core), 2 * (shift - m) + member - core))
        self.chain_left = bit(CHAIN_LEFT, m % 2, member, r, core)
        self.chain_right = bit(CHAIN_RIGHT, r % 2, member, m, core)
        self.shared = jnp.logical_not(jnp.logical_or(self.chain_left, self.chain_right))


def kernel(rows_n, cols_n, pattern, own, out, left, right, relay, total, left_recv, right_recv, relay_recv, send_sem, out_sem):
    r = lax.axis_index("row")
    c = lax.axis_index("col")
    chips = cols_n // 2
    m = c // 2
    core = c % 2

    barrier = pltpu.get_barrier_semaphore()
    for step in range(1, cols_n):
        pl.semaphore_signal(barrier, inc=1, device_id=(r, (c + step) % cols_n), device_id_type=MESH)
    for step in range(1, rows_n):
        pl.semaphore_signal(barrier, inc=1, device_id=((r + step) % rows_n, c), device_id_type=MESH)
    partner = r + 1 - 2 * (r % 2)
    for step in range(1, cols_n):
        pl.semaphore_signal(barrier, inc=1, device_id=(partner, (c + step) % cols_n), device_id_type=MESH)
    pl.semaphore_wait(barrier, 2 * cols_n + rows_n - 3)

    def rows_of(chunk, base=0):
        return pl.ds(pl.multiple_of(base + chunk * CR, CR), CR)

    def own_part(member, chunk):
        return own.at[rows_of(chunk, member * PB)]

    def left_part(slot, chunk):
        return left.at[slot, rows_of(chunk)]

    def right_part(slot, chunk):
        return right.at[slot, rows_of(chunk)]

    def relay_part(member, chunk):
        return relay.at[member, rows_of(chunk)]

    def remote(source, target, arrived, flow, device):
        return pltpu.make_async_remote_copy(
            src_ref=source, dst_ref=target, send_sem=send_sem.at[flow], recv_sem=arrived,
            device_id=device, device_id_type=MESH,
        )

    def is_here(device):
        return jnp.logical_and(device[0] == r, device[1] == c)

    def send(source, target, arrived, flow, device):
        here = is_here(device)

        @pl.when(here)
        def _():
            pltpu.make_async_copy(source, target, arrived).start()

        @pl.when(jnp.logical_not(here))
        def _():
            remote(source, target, arrived, flow, device).start()

    def send_left(source, way, far, chunk, flow):
        _, device, slot = way.left[far]
        send(source, left_part(slot, chunk), left_recv.at[slot, chunk], flow, device)

    def send_right(source, way, far, chunk, flow):
        _, device, slot = way.right[far]
        send(source, right_part(slot, chunk), right_recv.at[slot, chunk], flow, device)

    def wait(part, arrived):
        pltpu.make_async_copy(part, part, arrived).wait()

    mine = [Way(r, m, core, member, rows_n, chips) for member in range(2)]
    passing = [Way(partner, m, core, member, rows_n, chips) for member in range(2)]
    near_left = []
    for member in range(2):
        home_core = core if member == 0 else jnp.where(r % 2 == 0, 1 - core, core)
        shift = near_far(r + (1 - home_core) if member == 1 else r)[0]
        near_left.append(Way(r, (m + shift) % chips, home_core, member, rows_n, chips))
    near_right = []
    for member in range(2):
        shift = near_far(m + core if member == 0 else m)[0]
        near_right.append(Way((r + shift) % rows_n, m, core, member, rows_n, chips))

    def flow(member, kind):
        return member * 9 + kind

    def first(chunk, carry):
        for member, way in enumerate(mine):
            source = own_part(member, chunk)

            @pl.when(way.shared)
            def _(member=member, source=source):
                remote(source, relay_part(member, chunk), relay_recv.at[member, chunk], flow(member, 0), (partner, c)).start()

            @pl.when(jnp.logical_and(way.chain_right, jnp.logical_not(way.chain_left)))
            def _(member=member, source=source, way=way):
                send_left(source, way, 1, chunk, flow(member, 3))

            @pl.when(jnp.logical_and(way.chain_left, jnp.logical_not(way.chain_right)))
            def _(member=member, source=source, way=way):
                send_right(source, way, 1, chunk, flow(member, 4))

            send_right(source, way, 0, chunk, flow(member, 1))
            send_left(source, way, 0, chunk, flow(member, 2))
        return carry

    lax.fori_loop(0, CHUNKS, first, 0)

    def onward(chunk, carry):
        for member, way in enumerate(passing):
            @pl.when(way.shared)
            def _(member=member, way=way):
                source = relay_part(member, chunk)
                wait(source, relay_recv.at[member, chunk])
                send_right(source, way, 1, chunk, flow(member, 5))
                send_left(source, way, 1, chunk, flow(member, 6))

        for member, way in enumerate(near_right):
            slot = way.right[0][2]
            wait(right_part(slot, chunk), right_recv.at[slot, chunk])

            @pl.when(way.chain_right)
            def _(member=member, way=way, slot=slot):
                send_right(right_part(slot, chunk), way, 1, chunk, flow(member, 8))

        for member, way in enumerate(near_left):
            slot = way.left[0][2]
            wait(left_part(slot, chunk), left_recv.at[slot, chunk])

            @pl.when(way.chain_left)
            def _(member=member, way=way, slot=slot):
                send_left(left_part(slot, chunk), way, 1, chunk, flow(member, 7))
        return carry

    lax.fori_loop(0, CHUNKS, onward, 0)

    sibling = (r, c + 1 - 2 * core)
    crossing = ((jnp.where(core == 0, 2, 0), 1), (4, 3 + 2 * core))
    arriving = jnp.where(core == 0, 3, 5)
    far_left = (2 * (1 - r % 2), jnp.where(r % 2 == 0, 4, arriving))

    def across(chunk, carry):
        for slot in far_left:
            wait(left_part(slot, chunk), left_recv.at[slot, chunk])
        for index, (source, target) in enumerate(crossing):
            remote(left_part(source, chunk), left_part(target, chunk), left_recv.at[target, chunk], 18 + index, sibling).start()
        return carry

    lax.fori_loop(0, CHUNKS, across, 0)

    def arrived_right(chunk, carry):
        for way in near_right:
            slot = (way.right[0][2] + 2) % 4
            wait(right_part(slot, chunk), right_recv.at[slot, chunk])
        return carry

    lax.fori_loop(0, CHUNKS, arrived_right, 0)

    def multiply(chunk, carry):
        for slot in (1, 8 - arriving):
            wait(left_part(slot, chunk), left_recv.at[slot, chunk])
        for member in range(2):
            panel_row = 2 * r + member

            def row(step_row, carry, member=member, panel_row=panel_row):
                a = chunk * CR + step_row
                line = panel_row * PB + a
                goals = [pattern[line, 2 * c + e] for e in range(2)]
                acc = jnp.zeros((BS, 2 * BS), jnp.float32)
                for step in range(STEPS):
                    inner = (panel_row + c + step) % cols_n
                    slot = member * STEPS + step
                    lhs = jnp.concatenate([left[slot, a, 0], left[slot, a, 1]], axis=1)
                    parts = []
                    for f in range(2):
                        pick = pattern[line, 2 * inner + f]
                        held = [pattern[inner * PB + pick, 2 * c + g] for g in range(2)]
                        blocks = [right[member + step, pick, g] for g in range(2)]
                        zero = jnp.zeros_like(blocks[0])
                        parts.append(jnp.concatenate(
                            [jnp.where(held[0] == goals[e], blocks[0], jnp.where(held[1] == goals[e], blocks[1], zero)) for e in range(2)],
                            axis=1))
                    acc = acc + jnp.dot(lhs, jnp.concatenate(parts, axis=0), preferred_element_type=jnp.float32)
                total[member * PB + a, 0] = acc[:, :BS]
                total[member * PB + a, 1] = acc[:, BS:]
                return carry

            lax.fori_loop(0, CR, row, 0)
            part = rows_of(chunk, member * PB)
            pltpu.make_async_copy(total.at[part], out.at[part], out_sem.at[member]).start()
        return carry

    lax.fori_loop(0, CHUNKS, multiply, 0)

    def sent(number, condition):
        @pl.when(condition)
        def _():
            remote(left.at[0], left.at[0], left_recv.at[0, 0], number, sibling).wait_send()

    def away(device):
        return jnp.logical_not(is_here(device))

    for member in range(2):
        way, via = mine[member], passing[member]
        lonely_left = jnp.logical_and(way.chain_left, jnp.logical_not(way.chain_right))
        lonely_right = jnp.logical_and(way.chain_right, jnp.logical_not(way.chain_left))
        sent(flow(member, 0), way.shared)
        sent(flow(member, 1), away(way.right[0][1]))
        sent(flow(member, 2), away(way.left[0][1]))
        sent(flow(member, 3), jnp.logical_and(lonely_right, away(way.left[1][1])))
        sent(flow(member, 4), jnp.logical_and(lonely_left, away(way.right[1][1])))
        sent(flow(member, 5), jnp.logical_and(via.shared, away(via.right[1][1])))
        sent(flow(member, 6), jnp.logical_and(via.shared, away(via.left[1][1])))
        sent(flow(member, 7), jnp.logical_and(near_left[member].chain_left, away(near_left[member].left[1][1])))
        sent(flow(member, 8), jnp.logical_and(near_right[member].chain_right, away(near_right[member].right[1][1])))
    for index in range(2):
        remote(left.at[0], left.at[0], left_recv.at[0, 0], 18 + index, sibling).wait_send()
    for member in range(2):
        half = pl.ds(member * PB, PB)
        pltpu.make_async_copy(total.at[half], out.at[half], out_sem.at[member]).wait()


def solution(mesh):
    rows_n, cols_n = mesh.shape["row"], mesh.shape["col"]

    def shards(blocks, columns):
        def body(*refs):
            kernel(rows_n, cols_n, *refs)

        return pl.pallas_call(
            body,
            out_shape=jax.ShapeDtypeStruct(blocks.shape, jnp.float32),
            in_specs=[pl.BlockSpec(memory_space=pltpu.SMEM), pl.BlockSpec(memory_space=pl.ANY)],
            out_specs=pl.BlockSpec(memory_space=pl.ANY),
            scratch_shapes=[
                pltpu.VMEM((6, PB, 2, BS, BS), jnp.bfloat16),
                pltpu.VMEM((4, PB, 2, BS, BS), jnp.bfloat16),
                pltpu.VMEM((2, PB, 2, BS, BS), jnp.bfloat16),
                pltpu.VMEM((2 * PB, 2, BS, BS), jnp.float32),
                pltpu.SemaphoreType.DMA((6, CHUNKS)),
                pltpu.SemaphoreType.DMA((4, CHUNKS)),
                pltpu.SemaphoreType.DMA((2, CHUNKS)),
                pltpu.SemaphoreType.DMA((20,)),
                pltpu.SemaphoreType.DMA((2,)),
            ],
            compiler_params=pltpu.CompilerParams(
                collective_id=0, has_side_effects=True, vmem_limit_bytes=56 * 2**20
            ),
        )(columns, blocks)

    return jax.shard_map(
        shards, mesh=mesh, in_specs=(P("row", "col", None, None), P()),
        out_specs=P("row", "col", None, None), check_vma=False,
    )
```

time: 229 us -> 210 us (0.917)
  the two profiles are of different devices: /device:TPU:16 before, /device:TPU:41 now
where the time goes in v2:
time: 210 us; the launch traced here: 209 us
  Pallas kernels  200 us (95%)
  local copies, waits for them, and re-layouts  9.56 us (5%)
    pallas_call x1, Pallas kernels, shards(): pl.pallas_call(body, out_shape=jax.ShapeDtypeStruct(blocks.shape, jnp.flo...  200 us
    unnamed x2, local copies, waits for them, and re-layouts  9.56 us

profile of v2, /device:TPU:41, one launch (start us, length us, event | category | flops | bytes accessed | tf_op | source)
XLA Modules:
  0.0 209.5 jit_solution(296274876235845322)
XLA Ops:
  0.0 1.7 copy.3.refs_0_
  1.7 199.9 %shard_map.28 = f32[64,2,128,128]{3,2,1,0:T(8,128)} custom-call(s32[512,32]{1,0:T(8,128)} %copy.3.refs_0_, bf16[64,2,128,128]{3,2,1,0:T(8,128)(2,1)} %refs_1_.1), custom_call_target="tpu_custom_call" | custom-call | tf_op jit(solution)/shard_map/pallas_call | solution.py:266
  201.6 7.9 %copy.5 = f32[64,2,128,128]{3,2,1,0:T(8,128)} copy(f32[64,2,128,128]{3,2,1,0:T(8,128)} %shard_map.28) | data formatting | bytes 16777216

commit v3 on v2

--- a/solution.py
+++ b/solution.py
@@ -10,6 +10,7 @@
 BS = 128
 CHUNKS = 8
 CR = PB // CHUNKS
+LAG = 0
 MESH = pl.DeviceIdType.MESH
 
 CHAIN_LEFT = ((2952, 152), (400, 9824))
@@ -42,7 +43,7 @@
         self.shared = jnp.logical_not(jnp.logical_or(self.chain_left, self.chain_right))
 
 
-def kernel(rows_n, cols_n, pattern, own, out, left, right, relay, total, left_recv, right_recv, relay_recv, send_sem, out_sem):
+def kernel(rows_n, cols_n, pattern, own, total, left, right, relay, left_recv, right_recv, relay_recv, send_sem):
     r = lax.axis_index("row")
     c = lax.axis_index("col")
     chips = cols_n // 2
@@ -151,24 +152,45 @@
                 send_right(source, way, 1, chunk, flow(member, 5))
                 send_left(source, way, 1, chunk, flow(member, 6))
 
+        @pl.when(chunk >= LAG)
+        def _():
+            chained(chunk - LAG)
+        return carry
+
+    def chained(chunk):
         for member, way in enumerate(near_right):
-            slot = way.right[0][2]
-            wait(right_part(slot, chunk), right_recv.at[slot, chunk])
-
             @pl.when(way.chain_right)
-            def _(member=member, way=way, slot=slot):
+            def _(member=member, way=way):
+                slot = way.right[0][2]
+                wait(right_part(slot, chunk), right_recv.at[slot, chunk])
                 send_right(right_part(slot, chunk), way, 1, chunk, flow(member, 8))
 
         for member, way in enumerate(near_left):
-            slot = way.left[0][2]
-            wait(left_part(slot, chunk), left_recv.at[slot, chunk])
-
             @pl.when(way.chain_left)
-            def _(member=member, way=way, slot=slot):
+            def _(member=member, way=way):
+                slot = way.left[0][2]
+                wait(left_part(slot, chunk), left_recv.at[slot, chunk])
                 send_left(left_part(slot, chunk), way, 1, chunk, flow(member, 7))
-        return carry
 
     lax.fori_loop(0, CHUNKS, onward, 0)
+    for chunk in range(CHUNKS - LAG, CHUNKS):
+        chained(chunk)
+
+    def arrived_near(chunk, carry):
+        for way in near_right:
+            @pl.when(jnp.logical_not(way.chain_right))
+            def _(way=way):
+                slot = way.right[0][2]
+                wait(right_part(slot, chunk), right_recv.at[slot, chunk])
+
+        for way in near_left:
+            @pl.when(jnp.logical_not(way.chain_left))
+            def _(way=way):
+                slot = way.left[0][2]
+                wait(left_part(slot, chunk), left_recv.at[slot, chunk])
+        return carry
+
+    lax.fori_loop(0, CHUNKS, arrived_near, 0)
 
     sibling = (r, c + 1 - 2 * core)
     crossing = ((jnp.where(core == 0, 2, 0), 1), (4, 3 + 2 * core))
@@ -195,11 +217,10 @@
     def multiply(chunk, carry):
         for slot in (1, 8 - arriving):
             wait(left_part(slot, chunk), left_recv.at[slot, chunk])
-        for member in range(2):
-            panel_row = 2 * r + member
-
-            def row(step_row, carry, member=member, panel_row=panel_row):
-                a = chunk * CR + step_row
+        def row(step_row, carry):
+            a = chunk * CR + step_row
+            for member in range(2):
+                panel_row = 2 * r + member
                 line = panel_row * PB + a
                 goals = [pattern[line, 2 * c + e] for e in range(2)]
                 acc = jnp.zeros((BS, 2 * BS), jnp.float32)
@@ -219,11 +240,9 @@
                     acc = acc + jnp.dot(lhs, jnp.concatenate(parts, axis=0), preferred_element_type=jnp.float32)
                 total[member * PB + a, 0] = acc[:, :BS]
                 total[member * PB + a, 1] = acc[:, BS:]
-                return carry
-
-            lax.fori_loop(0, CR, row, 0)
-            part = rows_of(chunk, member * PB)
-            pltpu.make_async_copy(total.at[part], out.at[part], out_sem.at[member]).start()
+            return carry
+
+        lax.fori_loop(0, CR, row, 0, unroll=True)
         return carry
 
     lax.fori_loop(0, CHUNKS, multiply, 0)
@@ -251,9 +270,6 @@
         sent(flow(member, 8), jnp.logical_and(near_right[member].chain_right, away(near_right[member].right[1][1])))
     for index in range(2):
         remote(left.at[0], left.at[0], left_recv.at[0, 0], 18 + index, sibling).wait_send()
-    for member in range(2):
-        half = pl.ds(member * PB, PB)
-        pltpu.make_async_copy(total.at[half], out.at[half], out_sem.at[member]).wait()
 
 
 def solution(mesh):
@@ -267,20 +283,18 @@
             body,
             out_shape=jax.ShapeDtypeStruct(blocks.shape, jnp.float32),
             in_specs=[pl.BlockSpec(memory_space=pltpu.SMEM), pl.BlockSpec(memory_space=pl.ANY)],
-            out_specs=pl.BlockSpec(memory_space=pl.ANY),
+            out_specs=pl.BlockSpec(memory_space=pltpu.VMEM),
             scratch_shapes=[
                 pltpu.VMEM((6, PB, 2, BS, BS), jnp.bfloat16),
                 pltpu.VMEM((4, PB, 2, BS, BS), jnp.bfloat16),
                 pltpu.VMEM((2, PB, 2, BS, BS), jnp.bfloat16),
-                pltpu.VMEM((2 * PB, 2, BS, BS), jnp.float32),
                 pltpu.SemaphoreType.DMA((6, CHUNKS)),
                 pltpu.SemaphoreType.DMA((4, CHUNKS)),
                 pltpu.SemaphoreType.DMA((2, CHUNKS)),
                 pltpu.SemaphoreType.DMA((20,)),
-                pltpu.SemaphoreType.DMA((2,)),
             ],
             compiler_params=pltpu.CompilerParams(
-                collective_id=0, has_side_effects=True, vmem_limit_bytes=56 * 2**20
+                collective_id=0, has_side_effects=True, vmem_limit_bytes=40 * 2**20
             ),
         )(columns, blocks)
 

time: 210 us -> 192 us (0.914)
  Pallas kernels: 200 us -> 185 us
  local copies, waits for them, and re-layouts: 9.56 us -> 6.54 us
    pallas_call x1, Pallas kernels: 200 us -> 185 us  [shards(): pl.pallas_call(body, out_shape=jax.ShapeDtypeStruct(blocks.shape, jnp.flo...]
    unnamed x2 -> x4, local copies, waits for them, and re-layouts: 9.56 us -> 6.54 us
where the time goes in v3:
time: 192 us; the launch traced here: 191 us
  Pallas kernels  185 us (96%)
  local copies, waits for them, and re-layouts  6.54 us (3%)
    pallas_call x1, Pallas kernels, shards(): pl.pallas_call(body, out_shape=jax.ShapeDtypeStruct(blocks.shape, jnp.flo...  185 us
    unnamed x4, local copies, waits for them, and re-layouts  6.54 us

profile of v3, /device:TPU:41, one launch (start us, length us, event | category | flops | bytes accessed | tf_op | source)
XLA Modules:
  0.0 191.4 jit_solution(11532914604349305258)
XLA Ops:
  0.0 1.0 copy.3.refs_0_
  1.0 0.0 copy-start
  1.0 2.2 %copy-done = bf16[64,2,128,128]{3,2,1,0:T(8,128)(2,1)S(1)} copy-done((bf16[64,2,128,128]{3,2,1,0:T(8,128)(2,1)S(1)}, bf16[64,2,128,128]{3,2,1,0:T(8,128)(2,1)}, u32[]{:S(2)}) %copy-start) | copy-done | bytes 4194328
  3.2 184.8 %shard_map.28 = f32[64,2,128,128]{3,2,1,0:T(8,128)S(1)} custom-call(s32[512,32]{1,0:T(8,128)S(1)} %copy.3.refs_0_, bf16[64,2,128,128]{3,2,1,0:T(8,128)(2,1)S(1)} %copy-done), custom_call_target="tpu_custom_call" | custom-call | tf_op jit(solution)/shard_map/pallas_call | solution.py:282
  188.0 3.4 %copy.5 = f32[64,2,128,128]{3,2,1,0:T(8,128)} copy(f32[64,2,128,128]{3,2,1,0:T(8,128)S(1)} %shard_map.28) | data formatting | bytes 16777216
Async XLA Ops:
  1.0 2.2 %copy-start = (bf16[64,2,128,128]{3,2,1,0:T(8,128)(2,1)S(1)}, bf16[64,2,128,128]{3,2,1,0:T(8,128)(2,1)}, u32[]{:S(2)}) copy-start(bf16[64,2,128,128]{3,2,1,0:T(8,128)(2,1)} %refs_1_.1) | copy-start | bytes 12582916

commit v4 on v3

--- a/solution.py
+++ b/solution.py
@@ -13,13 +13,25 @@
 LAG = 0
 MESH = pl.DeviceIdType.MESH
 
-CHAIN_LEFT = ((2952, 152), (400, 9824))
-CHAIN_RIGHT = ((356, 2184), (2208, 8800))
+CHAIN_LEFT = ((1092, 33688), (37264, 1360))
+CHAIN_RIGHT = ((1092, 4948), (4496, 608))
+TURN_LEFT = (((16, 0), (0, 0)), ((0, 0), (1024, 512)))
+TURN_RIGHT = (((48, 0), (0, 0)), ((0, 0), (1024, 2304)))
 
 
 def bit(masks, parity, member, position, core):
     mask = jnp.where(parity == 0, masks[0][member], masks[1][member])
     return jnp.bitwise_and(jnp.right_shift(mask, position * 2 + core), 1) == 1
+
+
+def turn(masks, parity, member, position, core):
+    return jnp.where(bit(masks[0], parity, member, position, core), 1, jnp.where(bit(masks[1], parity, member, position, core), -1, 0))
+
+
+def halfway(start, end, around, direction):
+    natural = 1 - 2 * (start % 2)
+    opposite = (end - start + around) % around == around // 2
+    return jnp.logical_and(opposite, direction == -natural), (start + direction + around) % around
 
 
 def near_far(start):
@@ -41,9 +53,15 @@
         self.chain_left = bit(CHAIN_LEFT, m % 2, member, r, core)
         self.chain_right = bit(CHAIN_RIGHT, r % 2, member, m, core)
         self.shared = jnp.logical_not(jnp.logical_or(self.chain_left, self.chain_right))
-
-
-def kernel(rows_n, cols_n, pattern, own, total, left, right, relay, left_recv, right_recv, relay_recv, send_sem):
+        far = self.left[1][1][1]
+        stops, stop = halfway(m // 2, far // 4, chips // 2, turn(TURN_LEFT, m % 2, member, r, core))
+        self.stop_left, self.left_stop = jnp.logical_and(self.shared, stops), (r, stop * 4 + far % 4)
+        far = self.right[1][1][0]
+        stops, stop = halfway(r // 2, far // 2, rows_n // 2, turn(TURN_RIGHT, r % 2, member, m, core))
+        self.stop_right, self.right_stop = jnp.logical_and(self.shared, stops), (stop * 2 + far % 2, 2 * m + core)
+
+
+def kernel(rows_n, cols_n, pattern, own, total, left, right, relay, stop_left, stop_right, left_recv, right_recv, relay_recv, stop_left_recv, stop_right_recv, send_sem):
     r = lax.axis_index("row")
     c = lax.axis_index("col")
     chips = cols_n // 2
@@ -74,6 +92,9 @@
 
     def relay_part(member, chunk):
         return relay.at[member, rows_of(chunk)]
+
+    def stop_part(buffer, member, chunk):
+        return buffer.at[member, rows_of(chunk)]
 
     def remote(source, target, arrived, flow, device):
         return pltpu.make_async_remote_copy(
@@ -118,6 +139,16 @@
         shift = near_far(m + core if member == 0 else m)[0]
         near_right.append(Way((r + shift) % rows_n, m, core, member, rows_n, chips))
 
+    stopping_left, stopping_right = [], []
+    for member in range(2):
+        home_core = core if member == 0 else jnp.where(r % 2 == 0, core, 1 - core)
+        direction = turn(TURN_LEFT, 1 - m % 2, member, r, home_core)
+        home = (m // 2 - direction + chips // 2) % (chips // 2) * 2 + 1 - m % 2
+        stopping_left.append(Way(r, home, home_core, member, rows_n, chips))
+        direction = turn(TURN_RIGHT, 1 - r % 2, member, m, core)
+        home = (r // 2 - direction + rows_n // 2) % (rows_n // 2) * 2 + 1 - r % 2
+        stopping_right.append(Way(home, m, core, member, rows_n, chips))
+
     def flow(member, kind):
         return member * 9 + kind
 
@@ -149,13 +180,47 @@
             def _(member=member, way=way):
                 source = relay_part(member, chunk)
                 wait(source, relay_recv.at[member, chunk])
-                send_right(source, way, 1, chunk, flow(member, 5))
-                send_left(source, way, 1, chunk, flow(member, 6))
+
+                @pl.when(way.stop_right)
+                def _():
+                    remote(source, stop_part(stop_right, member, chunk), stop_right_recv.at[member, chunk], flow(member, 5), way.right_stop).start()
+
+                @pl.when(jnp.logical_not(way.stop_right))
+                def _():
+                    send_right(source, way, 1, chunk, flow(member, 5))
+
+                @pl.when(way.stop_left)
+                def _():
+                    remote(source, stop_part(stop_left, member, chunk), stop_left_recv.at[member, chunk], flow(member, 6), way.left_stop).start()
+
+                @pl.when(jnp.logical_not(way.stop_left))
+                def _():
+                    send_left(source, way, 1, chunk, flow(member, 6))
+
+        chained(chunk)
 
         @pl.when(chunk >= LAG)
         def _():
-            chained(chunk - LAG)
-        return carry
+            stopped(chunk - LAG)
+        return carry
+
+    def stopped(chunk):
+        for member in range(2):
+            way = stopping_right[member]
+
+            @pl.when(way.stop_right)
+            def _(member=member, way=way):
+                source = stop_part(stop_right, member, chunk)
+                wait(source, stop_right_recv.at[member, chunk])
+                send_right(source, way, 1, chunk, 18 + member)
+
+            way = stopping_left[member]
+
+            @pl.when(way.stop_left)
+            def _(member=member, way=way):
+                source = stop_part(stop_left, member, chunk)
+                wait(source, stop_left_recv.at[member, chunk])
+                send_left(source, way, 1, chunk, 20 + member)
 
     def chained(chunk):
         for member, way in enumerate(near_right):
@@ -174,7 +239,7 @@
 
     lax.fori_loop(0, CHUNKS, onward, 0)
     for chunk in range(CHUNKS - LAG, CHUNKS):
-        chained(chunk)
+        stopped(chunk)
 
     def arrived_near(chunk, carry):
         for way in near_right:
@@ -201,7 +266,7 @@
         for slot in far_left:
             wait(left_part(slot, chunk), left_recv.at[slot, chunk])
         for index, (source, target) in enumerate(crossing):
-            remote(left_part(source, chunk), left_part(target, chunk), left_recv.at[target, chunk], 18 + index, sibling).start()
+            remote(left_part(source, chunk), left_part(target, chunk), left_recv.at[target, chunk], 22 + index, sibling).start()
         return carry
 
     lax.fori_loop(0, CHUNKS, across, 0)
@@ -264,12 +329,14 @@
         sent(flow(member, 2), away(way.left[0][1]))
         sent(flow(member, 3), jnp.logical_and(lonely_right, away(way.left[1][1])))
         sent(flow(member, 4), jnp.logical_and(lonely_left, away(way.right[1][1])))
-        sent(flow(member, 5), jnp.logical_and(via.shared, away(via.right[1][1])))
-        sent(flow(member, 6), jnp.logical_and(via.shared, away(via.left[1][1])))
+        sent(flow(member, 5), jnp.logical_and(via.shared, jnp.logical_or(via.stop_right, away(via.right[1][1]))))
+        sent(flow(member, 6), jnp.logical_and(via.shared, jnp.logical_or(via.stop_left, away(via.left[1][1]))))
+        sent(18 + member, stopping_right[member].stop_right)
+        sent(20 + member, stopping_left[member].stop_left)
         sent(flow(member, 7), jnp.logical_and(near_left[member].chain_left, away(near_left[member].left[1][1])))
         sent(flow(member, 8), jnp.logical_and(near_right[member].chain_right, away(near_right[member].right[1][1])))
     for index in range(2):
-        remote(left.at[0], left.at[0], left_recv.at[0, 0], 18 + index, sibling).wait_send()
+        remote(left.at[0], left.at[0], left_recv.at[0, 0], 22 + index, sibling).wait_send()
 
 
 def solution(mesh):
@@ -288,13 +355,17 @@
                 pltpu.VMEM((6, PB, 2, BS, BS), jnp.bfloat16),
                 pltpu.VMEM((4, PB, 2, BS, BS), jnp.bfloat16),
                 pltpu.VMEM((2, PB, 2, BS, BS), jnp.bfloat16),
+                pltpu.VMEM((2, PB, 2, BS, BS), jnp.bfloat16),
+                pltpu.VMEM((2, PB, 2, BS, BS), jnp.bfloat16),
                 pltpu.SemaphoreType.DMA((6, CHUNKS)),
                 pltpu.SemaphoreType.DMA((4, CHUNKS)),
                 pltpu.SemaphoreType.DMA((2, CHUNKS)),
-                pltpu.SemaphoreType.DMA((20,)),
+                pltpu.SemaphoreType.DMA((2, CHUNKS)),
+                pltpu.SemaphoreType.DMA((2, CHUNKS)),
+                pltpu.SemaphoreType.DMA((24,)),
             ],
             compiler_params=pltpu.CompilerParams(
-                collective_id=0, has_side_effects=True, vmem_limit_bytes=40 * 2**20
+                collective_id=0, has_side_effects=True, vmem_limit_bytes=36 * 2**20
             ),
         )(columns, blocks)
 

time: 192 us -> 188 us (0.979)
  the two profiles are of different devices: /device:TPU:41 before, /device:TPU:106 now
where the time goes in v4:
time: 188 us
  Pallas kernels  182 us (97%)
  local copies, waits for them, and re-layouts  6.54 us (3%)
    pallas_call x1, Pallas kernels, shards(): pl.pallas_call(body, out_shape=jax.ShapeDtypeStruct(blocks.shape, jnp.flo...  182 us
    unnamed x4, local copies, waits for them, and re-layouts  6.54 us

profile of v4, /device:TPU:106, one launch (start us, length us, event | category | flops | bytes accessed | tf_op | source)
XLA Modules:
  0.0 188.2 jit_solution(18013642924416388810)
XLA Ops:
  0.0 1.0 copy.3.refs_0_
  1.0 0.0 copy-start
  1.0 2.2 %copy-done = bf16[64,2,128,128]{3,2,1,0:T(8,128)(2,1)S(1)} copy-done((bf16[64,2,128,128]{3,2,1,0:T(8,128)(2,1)S(1)}, bf16[64,2,128,128]{3,2,1,0:T(8,128)(2,1)}, u32[]{:S(2)}) %copy-start) | copy-done | bytes 4194328
  3.2 181.6 %shard_map.28 = f32[64,2,128,128]{3,2,1,0:T(8,128)S(1)} custom-call(s32[512,32]{1,0:T(8,128)S(1)} %copy.3.refs_0_, bf16[64,2,128,128]{3,2,1,0:T(8,128)(2,1)S(1)} %copy-done), custom_call_target="tpu_custom_call" | custom-call | tf_op jit(solution)/shard_map/pallas_call | solution.py:349
  184.8 3.4 %copy.5 = f32[64,2,128,128]{3,2,1,0:T(8,128)} copy(f32[64,2,128,128]{3,2,1,0:T(8,128)S(1)} %shard_map.28) | data formatting | bytes 16777216
Async XLA Ops:
  1.0 2.2 %copy-start = (bf16[64,2,128,128]{3,2,1,0:T(8,128)(2,1)S(1)}, bf16[64,2,128,128]{3,2,1,0:T(8,128)(2,1)}, u32[]{:S(2)}) copy-start(bf16[64,2,128,128]{3,2,1,0:T(8,128)(2,1)} %refs_1_.1) | copy-start | bytes 12582916

commit v5 on v4

--- a/solution.py
+++ b/solution.py
@@ -10,13 +10,13 @@
 BS = 128
 CHUNKS = 8
 CR = PB // CHUNKS
-LAG = 0
+LAG = 1
 MESH = pl.DeviceIdType.MESH
 
-CHAIN_LEFT = ((1092, 33688), (37264, 1360))
-CHAIN_RIGHT = ((1092, 4948), (4496, 608))
-TURN_LEFT = (((16, 0), (0, 0)), ((0, 0), (1024, 512)))
-TURN_RIGHT = (((48, 0), (0, 0)), ((0, 0), (1024, 2304)))
+CHAIN_LEFT = ((1092, 7065), (4496, 9826))
+CHAIN_RIGHT = ((1092, 7064), (6545, 8804))
+TURN_LEFT = (((16, 4), (0, 1)), ((0, 0), (1024, 2048)))
+TURN_RIGHT = (((48, 16384), (0, 0)), ((0, 0), (1024, 0)))
 
 
 def bit(masks, parity, member, position, core):
@@ -169,10 +169,23 @@
                 send_right(source, way, 1, chunk, flow(member, 4))
 
             send_right(source, way, 0, chunk, flow(member, 1))
-            send_left(source, way, 0, chunk, flow(member, 2))
+
+            @pl.when(way.chain_left)
+            def _(member=member, source=source, way=way):
+                send_left(source, way, 0, chunk, flow(member, 2))
+        return carry
+
+    def second(chunk, carry):
+        for member, way in enumerate(mine):
+            source = own_part(member, chunk)
+
+            @pl.when(jnp.logical_not(way.chain_left))
+            def _(member=member, source=source, way=way):
+                send_left(source, way, 0, chunk, flow(member, 2))
         return carry
 
     lax.fori_loop(0, CHUNKS, first, 0)
+    lax.fori_loop(0, CHUNKS, second, 0)
 
     def onward(chunk, carry):
         for member, way in enumerate(passing):

time: 188 us -> 180 us (0.957)
  the two profiles are of different devices: /device:TPU:106 before, /device:TPU:43 now
where the time goes in v5:
time: 180 us
  Pallas kernels  173 us (96%)
  local copies, waits for them, and re-layouts  6.54 us (4%)
    pallas_call x1, Pallas kernels, shards(): pl.pallas_call(body, out_shape=jax.ShapeDtypeStruct(blocks.shape, jnp.flo...  173 us
    unnamed x4, local copies, waits for them, and re-layouts  6.54 us

profile of v5, /device:TPU:43, one launch (start us, length us, event | category | flops | bytes accessed | tf_op | source)
XLA Modules:
  0.0 179.9 jit_solution(16322911937498587432)
XLA Ops:
  0.0 1.0 copy.3.refs_0_
  1.0 0.0 copy-start
  1.0 2.2 %copy-done = bf16[64,2,128,128]{3,2,1,0:T(8,128)(2,1)S(1)} copy-done((bf16[64,2,128,128]{3,2,1,0:T(8,128)(2,1)S(1)}, bf16[64,2,128,128]{3,2,1,0:T(8,128)(2,1)}, u32[]{:S(2)}) %copy-start) | copy-done | bytes 4194328
  3.2 173.3 %shard_map.28 = f32[64,2,128,128]{3,2,1,0:T(8,128)S(1)} custom-call(s32[512,32]{1,0:T(8,128)S(1)} %copy.3.refs_0_, bf16[64,2,128,128]{3,2,1,0:T(8,128)(2,1)S(1)} %copy-done), custom_call_target="tpu_custom_call" | custom-call | tf_op jit(solution)/shard_map/pallas_call | solution.py:362
  176.5 3.4 %copy.5 = f32[64,2,128,128]{3,2,1,0:T(8,128)} copy(f32[64,2,128,128]{3,2,1,0:T(8,128)S(1)} %shard_map.28) | data formatting | bytes 16777216
Async XLA Ops:
  1.0 2.2 %copy-start = (bf16[64,2,128,128]{3,2,1,0:T(8,128)(2,1)S(1)}, bf16[64,2,128,128]{3,2,1,0:T(8,128)(2,1)}, u32[]{:S(2)}) copy-start(bf16[64,2,128,128]{3,2,1,0:T(8,128)(2,1)} %refs_1_.1) | copy-start | bytes 12582916
